TPU v7x, 256 devices: a whole 4x4x8 slice. The times are simulated.
256 devices in a mesh: segment: 2 (over core), expert: 32 (over y, z), tensor: 4 (over x).
Axes of the slice: x: 4, y: 4, z: 8, core: 2. Of those that a mesh axis runs over, the one named last changes fastest.
Arguments:
- activations: bfloat16 [2, 2048, 2560], P('segment', 'expert', 'tensor'), may hold values from -48 to 48
- expert_ids: int32 [2, 2048, 6], P(None, 'expert'), may hold values from 0 to 63, as said below
- route_weights: float32 [2, 2048, 6], P(None, 'expert'), may hold values from 0.05 to 1
- gain_dense: float32 [2560], replicated, may hold values from 0.25 to 1.75
- gain_expert: float32 [2560], replicated, may hold values from 0.25 to 1.75
- dense_gate: bfloat16 [2560, 6144], P('expert', 'tensor'), may hold values from -0.125 to 0.125
- dense_up: bfloat16 [2560, 6144], P('expert', 'tensor'), may hold values from -0.125 to 0.125
- dense_down: bfloat16 [2560, 6144], P('expert', 'tensor'), may hold values from -0.078125 to 0.078125
- expert_gate: bfloat16 [64, 2560, 1536], P('expert', None, 'tensor'), may hold values from -0.125 to 0.125
- expert_up: bfloat16 [64, 2560, 1536], P('expert', None, 'tensor'), may hold values from -0.125 to 0.125
- expert_down: bfloat16 [64, 1536, 2560], P('expert', 'tensor'), may hold values from -0.15625 to 0.15625
Outputs:
- sections: bfloat16 [2, 2, 2048, 2560], P('segment', None, 'expert', 'tensor')
Inputs may be any that keep to these rules, and one draw needn't show every extreme that they name: `expert_ids`: each token names 6 different experts. Split each micro-batch's tokens into blocks of 64 in order: no expert is named by more than 12 tokens of one block, and in every micro-batch one expert is named by exactly 12 tokens of every block.
All inputs are finite; a program needn't handle non-finite values.
Results may differ from a plain program's by a relative error of at most 0.009.
Values may be sent and summed in bfloat16 or wider, within the bound.
A program may use at most 128 MiB of HBM per device.

v0:
```python
import jax
import jax.numpy as jnp
from jax import lax
from jax.sharding import PartitionSpec as P

EPSILON = 1e-06


def shifted(block, axis, distance):
    devices = range(lax.axis_size(axis))
    route = [((i - distance) % len(devices), i) for i in devices]
    return lax.ppermute(block, axis, route)


def normalize(values, gain_row):
    inverse = lax.rsqrt(jnp.mean(values * values, axis=-1, keepdims=True) + EPSILON)
    return values * inverse * gain_row


def dense_prepare(micro_block, gain_dense):
    micro_count, tokens_here, quarter = micro_block.shape
    whole_rows = lax.all_gather(micro_block, "tensor", axis=2, tiled=True)
    full_width = whole_rows.shape[2]
    normed = normalize(whole_rows.astype(jnp.float32), gain_dense).astype(jnp.bfloat16)
    return normed.reshape(micro_count * tokens_here, full_width)


def dense_finish(micro_block, partial_value):
    micro_count, tokens_here, quarter = micro_block.shape
    summed = lax.psum_scatter(
        partial_value.reshape(micro_count, tokens_here, partial_value.shape[1]).astype(
            jnp.bfloat16
        ),
        "tensor",
        scatter_dimension=2,
        tiled=True,
    ).astype(jnp.float32)
    return (micro_block.astype(jnp.float32) + summed).astype(jnp.bfloat16)


def dense_folded(activations, gain_dense, dense_gate, dense_up, dense_down):
    normed = dense_prepare(activations, gain_dense)
    gate_sums = jnp.dot(
        normed,
        lax.all_gather(dense_gate, "expert", axis=0, tiled=True),
        preferred_element_type=jnp.float32,
    )
    upward = jnp.dot(
        normed,
        lax.all_gather(dense_up, "expert", axis=0, tiled=True),
        preferred_element_type=jnp.float32,
    )
    hidden = (jax.nn.silu(gate_sums) * upward).astype(jnp.bfloat16)
    partial_value = lax.dot_general(
        hidden,
        lax.all_gather(dense_down, "expert", axis=0, tiled=True),
        (((1,), (1,)), ((), ())),
        preferred_element_type=jnp.float32,
    )
    return dense_finish(activations, partial_value)


def route_slots(expert_ids_block, local_count, groups, capacity):
    tokens_here, picks = expert_ids_block.shape
    flat_ids = expert_ids_block.reshape(-1)
    experts_all = local_count * groups
    one_hot = (flat_ids[:, None] == jnp.arange(experts_all, dtype=jnp.int32)[None, :]).astype(
        jnp.int32
    )
    ranks = jnp.sum((jnp.cumsum(one_hot, axis=0) - 1) * one_hot, axis=1)
    slots = (flat_ids % local_count * groups + flat_ids // local_count) * capacity + ranks
    owners = jnp.arange(tokens_here * picks, dtype=jnp.int32) // picks
    sources = jnp.full((experts_all * capacity,), tokens_here, jnp.int32).at[slots].set(owners)
    return (slots, sources)


def place_rows(normed, sources, local_count, groups, capacity):
    padded = jnp.concatenate([normed, jnp.zeros((1, normed.shape[1]), normed.dtype)], axis=0)
    return padded[sources].reshape(local_count, groups, capacity, normed.shape[1])


def expert_block(
    middle, expert_ids_block, route_block, gain_expert, expert_gate, expert_up, expert_down
):
    tokens_here, quarter = middle.shape
    picks = expert_ids_block.shape[1]
    groups = lax.axis_size("expert")
    local_count, full_width, hidden_part = expert_gate.shape
    capacity = min(tokens_here, 2 * (tokens_here * picks // (local_count * groups)))
    slots, sources = route_slots(expert_ids_block, local_count, groups, capacity)
    middle_wide = middle.astype(jnp.float32)
    received_rows = groups * capacity
    tensor_index = lax.axis_index("tensor")
    square_sums = lax.psum(jnp.sum(middle_wide * middle_wide, axis=1), "tensor")
    inverse = lax.rsqrt(square_sums / full_width + EPSILON)
    gain_part = lax.dynamic_slice_in_dim(gain_expert, tensor_index * quarter, quarter, 0)
    normed = (middle_wide * inverse[:, None] * gain_part).astype(jnp.bfloat16)
    outgoing = place_rows(normed, sources, local_count, groups, capacity)
    arrived = lax.all_to_all(outgoing, "expert", split_axis=1, concat_axis=1, tiled=True)
    arrived = arrived.reshape(local_count, received_rows, quarter)
    slice_part = lax.all_gather(arrived, "tensor", axis=2, tiled=True)
    gate_sums = jnp.einsum(
        "lrc,lch->lrh", slice_part, expert_gate, preferred_element_type=jnp.float32
    )
    upward = jnp.einsum("lrc,lch->lrh", slice_part, expert_up, preferred_element_type=jnp.float32)
    hidden = (jax.nn.silu(gate_sums) * upward).astype(jnp.bfloat16)
    partial_value = jnp.einsum(
        "lrh,lhd->lrd", hidden, expert_down, preferred_element_type=jnp.float32
    )
    summed = lax.psum_scatter(
        partial_value.astype(jnp.bfloat16), "tensor", scatter_dimension=2, tiled=True
    )
    returned = lax.all_to_all(
        summed.reshape(local_count, groups, capacity, quarter),
        "expert",
        split_axis=1,
        concat_axis=1,
        tiled=True,
    )
    picked = returned.reshape(local_count * groups * capacity, quarter)[slots]
    picked = picked.reshape(tokens_here, picks, quarter).astype(jnp.float32)
    mixed = jnp.sum(route_block[:, :, None] * picked, axis=1)
    return (middle_wide + mixed).astype(jnp.bfloat16)


def body(
    activations,
    expert_ids,
    route_weights,
    gain_dense,
    gain_expert,
    dense_gate,
    dense_up,
    dense_down,
    expert_gate,
    expert_up,
    expert_down,
):
    segment_index = lax.axis_index("segment")
    own_middle = dense_folded(activations, gain_dense, dense_gate, dense_up, dense_down)
    other_middle = shifted(own_middle, "segment", 1)
    middles = jnp.where(
        segment_index == 0,
        jnp.concatenate([own_middle, other_middle], axis=0),
        jnp.concatenate([other_middle, own_middle], axis=0),
    )
    finals = jnp.stack(
        [
            expert_block(
                middles[position],
                expert_ids[position],
                route_weights[position],
                gain_expert,
                expert_gate,
                expert_up,
                expert_down,
            )
            for position in range(middles.shape[0])
        ]
    )
    sections = jnp.where(segment_index == 0, middles, finals)
    return sections[None]


def solution(mesh):
    placed = (
        P("segment", "expert", "tensor"),
        P(None, "expert", None),
        P(None, "expert", None),
        P(),
        P(),
        P("expert", "tensor"),
        P("expert", "tensor"),
        P("expert", "tensor"),
        P("expert", None, "tensor"),
        P("expert", None, "tensor"),
        P("expert", "tensor", None),
    )
    return jax.shard_map(
        body,
        mesh=mesh,
        in_specs=placed,
        out_specs=P("segment", None, "expert", "tensor"),
        check_vma=False,
    )
```

profile of v0, /device:TPU:32, one launch (start us, length us, event | category | flops | bytes accessed | tf_op | source)
XLA Modules:
  0.0 638.5 jit_solution(418148062136196478)
XLA Ops:
  11.0 13.0 %all_gather.18 = bf16[1,64,2560]{2,1,0:T(8,128)(2,1)S(1)} all-gather(bf16[1,64,640]{2,1,0:T(8,128)(2,1)} %param.11), channel_id=1, replica_groups=mesh['segment'=2,'expert'=32,'tensor'=4] {'tensor'}, dimensions={2}, use_global_device_ids=true | all-gather | bytes 409600 | tf_op jit(solution)/shard_map/all_gather | solution.py:22
  24.2 82.8 %all-gather.6.cloned.1.call-done = bf16[2560,1536]{1,0:T(8,128)(2,1)} async-done(((bf16[80,1536]{1,0:T(8,128)(2,1)}), bf16[2560,1536]{1,0:T(8,128)(2,1)}) %all-gather.6.cloned.1.call-update) | async-done | bytes 7864336 | tf_op jit(solution)/shard_map/all_gather | solution.py:45
  107.1 4.8 fusion.37
  111.9 90.8 %all-gather.10.cloned.1.call-done = bf16[2560,1536]{1,0:T(8,128)(2,1)} async-done(((bf16[80,1536]{1,0:T(8,128)(2,1)}), bf16[2560,1536]{1,0:T(8,128)(2,1)}) %all-gather.10.cloned.1.call-update) | async-done | bytes 7864336 | tf_op jit(solution)/shard_map/all_gather | solution.py:56
  202.7 95.6 %all-gather.8.cloned.1.call-done = bf16[2560,1536]{1,0:T(8,128)(2,1)} async-done(((bf16[80,1536]{1,0:T(8,128)(2,1)}), bf16[2560,1536]{1,0:T(8,128)(2,1)}) %all-gather.8.cloned.1.call-update) | async-done | bytes 7864336 | tf_op jit(solution)/shard_map/all_gather | solution.py:50
  298.3 9.4 %fusion = bf16[1,64,2560]{2,1,0:T(8,128)(2,1)S(1)} fusion(bf16[2560,1536]{1,0:T(8,128)(2,1)} %all-gather.10.cloned.1.call-done, bf16[2560,1536]{1,0:T(8,128)(2,1)} %all-gather.8.cloned.1.call-done, f32[64,1536]{1,0:T(8,128)S(1)} %fusion.37, bf16[1,64,2560]{2,1,0:T(8,128)(2,1)S(1)} %all_gather.18, f32[2560]{0:T(1024)S(1)} %copy-done.3, f32[64]{0:T(128)S(1)} %add_rsqrt_fusion.2), kind=kOutput, calls=%fused_computation.9 | convolution fusion | flops 1008041984 | bytes 16787712 | tf_op jit(solution)/shard_map/dot_general | solution.py:54
  311.4 2.9 scatter_custom_fusion.1
  314.3 18.2 %reduce-scatter.10.cloned.1.call-done = bf16[640,64]{1,0:T(8,128)(2,1)} async-done(((bf16[2560,64]{1,0:T(8,128)(2,1)}), bf16[640,64]{1,0:T(8,128)(2,1)}) %reduce-scatter.10.cloned.1.call-update) | async-done | bytes 81936
  336.0 8.4 %all-reduce.2 = (f32[64]{0:T(128)S(1)}, f32[64]{0:T(128)S(1)}) all-reduce(f32[64]{0:T(128)S(1)} %get-tuple-element.5, f32[64]{0:T(128)S(1)} %get-tuple-element.6), channel_id=1, replica_groups=mesh['segment'=2,'expert'=32,'tensor'=4] {'tensor'}, use_global_device_ids=true, to_apply=%region_3.4 | all-reduce | flops 128 | bytes 1024 | tf_op jit(solution)/shard_map/psum | solution.py:94
  344.5 2.8 gather_fusion.2
  348.6 35.7 %all_to_all.20 = bf16[2,32,12,640]{3,0,2,1:T(2,128)(2,1)S(1)} all-to-all(bf16[2,32,12,640]{3,0,2,1:T(2,128)(2,1)S(1)} %copy.50), channel_id=1, replica_groups=mesh['segment'=2,'expert'=32,'tensor'=4] {'expert'}, dimensions={1} | all-to-all | bytes 1966080 | tf_op jit(solution)/shard_map/all_to_all | solution.py:99
  387.9 3.1 scatter_custom_fusion
  391.1 2.8 gather_fusion
  395.1 29.5 %all_to_all.21 = bf16[2,32,12,640]{3,0,2,1:T(2,128)(2,1)S(1)} all-to-all(bf16[2,32,12,640]{3,0,2,1:T(2,128)(2,1)S(1)} %copy.40), channel_id=1, replica_groups=mesh['segment'=2,'expert'=32,'tensor'=4] {'expert'}, dimensions={1} | all-to-all | bytes 1966080 | tf_op jit(solution)/shard_map/all_to_all | solution.py:99
  425.8 2.8 all-gather.14.cloned.1.call-done
  428.7 5.5 fusion.60
  434.2 10.7 %convolution_convert_fusion = bf16[2,384,2560]{2,1,0:T(8,128)(2,1)} fusion(bf16[2,384,2560]{2,1,0:T(8,128)(2,1)} %param.21, bf16[2,384,2560]{2,1,0:T(8,128)(2,1)} %all-gather.14.cloned.1.call-done, bf16[2,2560,384]{2,1,0:T(8,128)(2,1)} %param.20, f32[2,384,384]{2,1,0:T(8,128)S(1)} %fusion.60), kind=kOutput, calls=%fused_computation.6 | convolution fusion | flops 3023634432 | bytes 16908288 | tf_op jit(solution)/shard_map/lrh,lhd->lrd/dot_general | solution.py:107
  444.8 10.6 %copy.58 = bf16[2,384,2560]{1,0,2:T(2,128)(2,1)} copy(bf16[2,384,2560]{2,1,0:T(8,128)(2,1)} %convolution_convert_fusion) | data formatting | bytes 7864320
  455.5 4.7 copy.70
  460.5 18.9 %all-gather.12.cloned.1.call-done = bf16[2,384,2560]{2,1,0:T(8,128)(2,1)} async-done(((bf16[2,384,640]{2,1,0:T(8,128)(2,1)}), bf16[2,384,2560]{2,1,0:T(8,128)(2,1)}) %all-gather.12.cloned.1.call-update) | async-done | bytes 3932176 | tf_op jit(solution)/shard_map/all_gather | solution.py:101
  479.4 5.5 fusion.59
  484.9 10.7 %convolution_convert_fusion.1 = bf16[2,384,2560]{2,1,0:T(8,128)(2,1)} fusion(bf16[2,384,2560]{2,1,0:T(8,128)(2,1)} %param.21, bf16[2,384,2560]{2,1,0:T(8,128)(2,1)} %all-gather.12.cloned.1.call-done, bf16[2,2560,384]{2,1,0:T(8,128)(2,1)} %param.20, f32[2,384,384]{2,1,0:T(8,128)S(1)} %fusion.59), kind=kOutput, calls=%fused_computation.7 | convolution fusion | flops 3023634432 | bytes 16908288 | tf_op jit(solution)/shard_map/lrh,lhd->lrd/dot_general | solution.py:107
  495.5 10.6 %copy.56 = bf16[2,384,2560]{1,0,2:T(2,128)(2,1)} copy(bf16[2,384,2560]{2,1,0:T(8,128)(2,1)} %convolution_convert_fusion.1) | data formatting | bytes 7864320
  506.1 4.7 copy.69
  510.8 18.7 %reduce-scatter.14.cloned.1.call-done = bf16[640,768]{1,0:T(8,128)(2,1)} async-done(((bf16[2560,768]{1,0:T(8,128)(2,1)}), bf16[640,768]{1,0:T(8,128)(2,1)}) %reduce-scatter.14.cloned.1.call-update) | async-done | bytes 983056
  531.8 2.8 copy.52
  534.6 10.2 %all-to-all-start.3 = ((bf16[2,32,12,640]{3,0,2,1:T(2,128)(2,1)}), bf16[2,32,12,640]{3,0,2,1:T(2,128)(2,1)S(1)}, u32[]{:S(2)}, u32[]{:S(2)}) async-start(bf16[2,32,12,640]{3,0,2,1:T(2,128)(2,1)} %bitcast.15), calls=%async_computation.3 | async-start | bytes 1966080 | tf_op jit(solution)/shard_map/all_to_all | solution.py:113
  544.9 34.2 %reduce-scatter.12.cloned.1.call-done = bf16[640,768]{1,0:T(8,128)(2,1)} async-done(((bf16[2560,768]{1,0:T(8,128)(2,1)}), bf16[640,768]{1,0:T(8,128)(2,1)}) %reduce-scatter.12.cloned.1.call-update) | async-done | bytes 983056
  581.3 2.9 copy.42
  584.2 10.1 %all-to-all-start.1 = ((bf16[2,32,12,640]{3,0,2,1:T(2,128)(2,1)}), bf16[2,32,12,640]{3,0,2,1:T(2,128)(2,1)S(1)}, u32[]{:S(2)}, u32[]{:S(2)}) async-start(bf16[2,32,12,640]{3,0,2,1:T(2,128)(2,1)} %bitcast.8), calls=%async_computation.1 | async-start | bytes 1966080 | tf_op jit(solution)/shard_map/all_to_all | solution.py:113
  596.8 2.8 gather_fusion.3
  600.7 20.8 %all-to-all-done.1 = bf16[2,32,12,640]{3,0,2,1:T(2,128)(2,1)S(1)} async-done(((bf16[2,32,12,640]{3,0,2,1:T(2,128)(2,1)}), bf16[2,32,12,640]{3,0,2,1:T(2,128)(2,1)S(1)}, u32[]{:S(2)}, u32[]{:S(2)}) %all-to-all-start.1) | async-done | bytes 983072 | tf_op jit(solution)/shard_map/all_to_all | solution.py:113
  (103 shorter events, 37.7 us)
Async XLA Ops:
  6.5 100.5 %all-gather.6.cloned.1.call-start = ((), (), s32[]{:S(2)}) async-start(), calls=%async_computation.7 | async-start | bytes 8110080 | tf_op jit(solution)/shard_map/all_gather | solution.py:45
  7.3 195.4 %all-gather.10.cloned.1.call-start = ((), (), s32[]{:S(2)}) async-start(), calls=%async_computation.9 | async-start | bytes 8110080 | tf_op jit(solution)/shard_map/all_gather | solution.py:56
  8.0 290.3 %all-gather.8.cloned.1.call-start = ((), (), s32[]{:S(2)}) async-start(), calls=%async_computation.8 | async-start | bytes 8110080 | tf_op jit(solution)/shard_map/all_gather | solution.py:50
  8.7 323.8 %reduce-scatter.10.cloned.1.call-start = ((), (), s32[]{:S(2)}) async-start(), calls=%async_computation.12 | async-start | bytes 819200
  24.2 274.0 %copy-start.3 = (f32[2560]{0:T(1024)S(1)}, f32[2560]{0:T(1024)}, u32[]{:S(2)}) copy-start(f32[2560]{0:T(1024)} %param.14) | copy-start | bytes 30724
  307.7 26.1 %copy-start.2 = (bf16[1,64,640]{2,1,0:T(8,128)(2,1)S(1)}, bf16[1,64,640]{2,1,0:T(8,128)(2,1)}, u32[]{:S(2)}) copy-start(bf16[1,64,640]{2,1,0:T(8,128)(2,1)} %param.11) | copy-start | bytes 245764
  309.6 119.1 %all-gather.14.cloned.1.call-start = ((), (), s32[]{:S(2)}) async-start(), calls=%async_computation.11 | async-start | bytes 4915200 | tf_op jit(solution)/shard_map/all_gather | solution.py:101
  310.8 0.6 copy-start.5
  333.8 1.4 collective-permute-start
  335.2 0.6 copy-start
  385.4 93.9 %all-gather.12.cloned.1.call-start = ((), (), s32[]{:S(2)}) async-start(), calls=%async_computation.10 | async-start | bytes 4915200 | tf_op jit(solution)/shard_map/all_gather | solution.py:101
  387.3 0.6 copy-start.7
  425.8 103.7 %reduce-scatter.14.cloned.1.call-start = ((), (), s32[]{:S(2)}) async-start(), calls=%async_computation.14 | async-start | bytes 4915200
  460.2 118.8 %reduce-scatter.12.cloned.1.call-start = ((), (), s32[]{:S(2)}) async-start(), calls=%async_computation.13 | async-start | bytes 4915200
  534.6 59.7 %copy-start.9 = (f32[2,64,6]{1,0,2:T(2,128)S(1)}, f32[2,64,6]{1,0,2:T(2,128)}, u32[]{:S(2)}) copy-start(f32[2,64,6]{1,0,2:T(2,128)} %param.13) | copy-start | bytes 9220
  534.6 60.5 %copy-start.6 = (s32[384]{0:T(512)S(1)}, s32[384]{0:T(512)}, u32[]{:S(2)}) copy-start(s32[384]{0:T(512)} %copy-done.5) | copy-start | bytes 4612
  534.6 61.1 %copy-start.8 = (s32[384]{0:T(512)S(1)}, s32[384]{0:T(512)}, u32[]{:S(2)}) copy-start(s32[384]{0:T(512)} %copy-done.7) | copy-start | bytes 4612
  534.6 49.6 %all-to-all-start.3 = ((bf16[2,32,12,640]{3,0,2,1:T(2,128)(2,1)}), bf16[2,32,12,640]{3,0,2,1:T(2,128)(2,1)S(1)}, u32[]{:S(2)}, u32[]{:S(2)}) async-start(bf16[2,32,12,640]{3,0,2,1:T(2,128)(2,1)} %bitcast.15), calls=%async_computation.3 | async-start | bytes 1966080 | tf_op jit(solution)/shard_map/all_to_all | solution.py:113
  584.2 37.3 %all-to-all-start.1 = ((bf16[2,32,12,640]{3,0,2,1:T(2,128)(2,1)}), bf16[2,32,12,640]{3,0,2,1:T(2,128)(2,1)S(1)}, u32[]{:S(2)}, u32[]{:S(2)}) async-start(bf16[2,32,12,640]{3,0,2,1:T(2,128)(2,1)} %bitcast.8), calls=%async_computation.1 | async-start | bytes 1966080 | tf_op jit(solution)/shard_map/all_to_all | solution.py:113
  624.9 4.1 copy-start.4
  624.9 6.0 copy-start.1
Sparse Core Ops, SparseCore 0:
  9.9 97.0 all-gather.5
  109.7 92.9 all-gather.9
  205.3 92.9 all-gather.7
  309.7 22.8 reduce-scatter.9
  385.6 43.0 all-gather.13
  430.4 48.9 all-gather.11
  481.9 47.5 reduce-scatter.13
  532.1 46.9 reduce-scatter.11
where the time goes:
time: 640 us; the launch traced here: 638 us
  waiting for transfers between devices  386 us (60%)
  blocking collectives  86.6 us (14%)
  local copies, waits for them, and re-layouts  77.5 us (12%)
  matrix products  46.4 us (7%)
  starting transfers between devices  20.9 us (3%)
  between operations  13.9 us (2%)
  other arithmetic  6.87 us (1%)
    all_gather x1, waiting for transfers between devices, dense_folded(): lax.all_gather(dense_up, 'expert', axis=0, tiled=True)  95.6 us
    all_gather x1, waiting for transfers between devices, dense_folded(): lax.all_gather(dense_down, 'expert', axis=0, tiled=True)  90.8 us
    all_gather x1, waiting for transfers between devices, dense_folded(): lax.all_gather(dense_gate, 'expert', axis=0, tiled=True)  82.8 us
    unnamed x11, waiting for transfers between devices  73.2 us
    all_to_all x2, blocking collectives, expert_block(): lax.all_to_all(outgoing, 'expert', split_axis=1, concat_axis=1, tiled=True)  65.2 us
    unnamed x30, local copies, waits for them, and re-layouts  40.2 us
    all_gather x2, waiting for transfers between devices, expert_block(): slice_part = lax.all_gather(arrived, 'tensor', axis=2, tiled=True)  21.7 us
    dot_general x2, matrix products, expert_block(): jnp.einsum('lrh,lhd->lrd', hidden, expert_down, preferred_element_type=jn...  21.3 us
  transfers between devices with their start and end apart: 11, of which 10 were waited for; matrix products, arithmetic and copies ran while one was open for 16% of the time, Pallas kernels for 0%

commit v1 on v0

--- a/solution.py
+++ b/solution.py
@@ -98,7 +98,23 @@
     outgoing = place_rows(normed, sources, local_count, groups, capacity)
     arrived = lax.all_to_all(outgoing, "expert", split_axis=1, concat_axis=1, tiled=True)
     arrived = arrived.reshape(local_count, received_rows, quarter)
-    slice_part = lax.all_gather(arrived, "tensor", axis=2, tiled=True)
+    ways, here, step = (lax.axis_size("tensor"), lax.axis_index("tensor"), arrived.shape[2])
+    dims = [n * ways if d == 2 else n for d, n in enumerate(arrived.shape)]
+    full = lax.dynamic_update_slice_in_dim(
+        jnp.zeros(dims, arrived.dtype), arrived, here * step, axis=2
+    )
+    going_up = going_down = arrived
+    for far in range(1, ways // 2 + 1):
+        going_up = lax.ppermute(going_up, "tensor", [(d, (d + 1) % ways) for d in range(ways)])
+        full = lax.dynamic_update_slice_in_dim(full, going_up, (here - far) % ways * step, axis=2)
+        if 2 * far < ways:
+            going_down = lax.ppermute(
+                going_down, "tensor", [(d, (d - 1) % ways) for d in range(ways)]
+            )
+            full = lax.dynamic_update_slice_in_dim(
+                full, going_down, (here + far) % ways * step, axis=2
+            )
+    slice_part = full
     gate_sums = jnp.einsum(
         "lrc,lch->lrh", slice_part, expert_gate, preferred_element_type=jnp.float32
     )

time: 640 us -> 690 us (1.078); the launches traced: 638 us -> 681 us
  waiting for transfers between devices: 386 us -> 421 us
  starting transfers between devices: 20.9 us -> 29.5 us
    ppermute x0 -> x6, waiting for transfers between devices: none -> 79.7 us  [the longest x4 79.7 us: expert_block(): lax.ppermute(going_up, 'tensor', [(d, (d + 1) % ways) for d in range(ways)])]
    all_gather x2 -> x0, waiting for transfers between devices: 21.7 us -> none  [expert_block(): slice_part = lax.all_gather(arrived, 'tensor', axis=2, tiled=True)]
    unnamed x11 -> x9, waiting for transfers between devices: 73.2 us -> 52.7 us
    ppermute x0 -> x6, starting transfers between devices: none -> 8.38 us  [the longest x2 5.07 us: expert_block(): lax.ppermute(going_down, 'tensor', [(d, (d - 1) % ways) for d in range(wa...]
    unnamed x30 -> x38, local copies, waits for them, and re-layouts: 40.2 us -> 43 us
  transfers between devices with their start and end apart: 11 -> 15, of which waited for: 10 -> 11; matrix products, arithmetic and copies ran while one was open for 16% -> 10% of each run, Pallas kernels for 0% -> 0%
where the time goes in v1:
time: 690 us; the launch traced here: 681 us
  waiting for transfers between devices  421 us (61%)
  blocking collectives  88.2 us (13%)
  local copies, waits for them, and re-layouts  81.3 us (12%)
  matrix products  39.6 us (6%)
  starting transfers between devices  29.5 us (4%)
  between operations  14.3 us (2%)
    all_gather x1, waiting for transfers between devices, dense_folded(): lax.all_gather(dense_down, 'expert', axis=0, tiled=True)  95.6 us
    all_gather x1, waiting for transfers between devices, dense_folded(): lax.all_gather(dense_up, 'expert', axis=0, tiled=True)  90.8 us
    all_gather x1, waiting for transfers between devices, dense_folded(): lax.all_gather(dense_gate, 'expert', axis=0, tiled=True)  80.1 us
    ppermute x4, waiting for transfers between devices, expert_block(): lax.ppermute(going_up, 'tensor', [(d, (d + 1) % ways) for d in range(ways)])  79.7 us
    all_to_all x2, blocking collectives, expert_block(): lax.all_to_all(outgoing, 'expert', split_axis=1, concat_axis=1, tiled=True)  66.8 us
    unnamed x9, waiting for transfers between devices  52.7 us
    unnamed x38, local copies, waits for them, and re-layouts  43 us
    dot_general x2, matrix products, expert_block(): jnp.einsum('lrh,lhd->lrd', hidden, expert_down, preferred_element_type=jn...  21.1 us
  transfers between devices with their start and end apart: 15, of which 11 were waited for; matrix products, arithmetic and copies ran while one was open for 10% of the time, Pallas kernels for 0%

profile of v1, /device:TPU:32, one launch (start us, length us, event | category | flops | bytes accessed | tf_op | source)
XLA Modules:
  0.0 680.5 jit_solution(17122669846106471444)
XLA Ops:
  13.8 13.0 %all_gather.12 = bf16[1,64,2560]{2,1,0:T(8,128)(2,1)S(1)} all-gather(bf16[1,64,640]{2,1,0:T(8,128)(2,1)} %param.11), channel_id=1, replica_groups=mesh['segment'=2,'expert'=32,'tensor'=4] {'tensor'}, dimensions={2}, use_global_device_ids=true | all-gather | bytes 409600 | tf_op jit(solution)/shard_map/all_gather | solution.py:22
  27.0 80.1 %all-gather.4.cloned.1.call-done = bf16[2560,1536]{1,0:T(8,128)(2,1)} async-done(((bf16[80,1536]{1,0:T(8,128)(2,1)}), bf16[2560,1536]{1,0:T(8,128)(2,1)}) %all-gather.4.cloned.1.call-update) | async-done | bytes 7864336 | tf_op jit(solution)/shard_map/all_gather | solution.py:45
  107.1 4.8 fusion.35
  111.9 90.8 %all-gather.6.cloned.1.call-done = bf16[2560,1536]{1,0:T(8,128)(2,1)} async-done(((bf16[80,1536]{1,0:T(8,128)(2,1)}), bf16[2560,1536]{1,0:T(8,128)(2,1)}) %all-gather.6.cloned.1.call-update) | async-done | bytes 7864336 | tf_op jit(solution)/shard_map/all_gather | solution.py:50
  202.7 95.6 %all-gather.8.cloned.1.call-done = bf16[2560,1536]{1,0:T(8,128)(2,1)} async-done(((bf16[80,1536]{1,0:T(8,128)(2,1)}), bf16[2560,1536]{1,0:T(8,128)(2,1)}) %all-gather.8.cloned.1.call-update) | async-done | bytes 7864336 | tf_op jit(solution)/shard_map/all_gather | solution.py:56
  298.3 9.4 %fusion = bf16[1,64,2560]{2,1,0:T(8,128)(2,1)S(1)} fusion(bf16[2560,1536]{1,0:T(8,128)(2,1)} %all-gather.8.cloned.1.call-done, bf16[2560,1536]{1,0:T(8,128)(2,1)} %all-gather.6.cloned.1.call-done, f32[64,1536]{1,0:T(8,128)S(1)} %fusion.35, bf16[1,64,2560]{2,1,0:T(8,128)(2,1)S(1)} %all_gather.12, f32[2560]{0:T(1024)S(1)} %copy-done.5, f32[64]{0:T(128)S(1)} %add_rsqrt_fusion.2), kind=kOutput, calls=%fused_computation.9 | convolution fusion | flops 1008041984 | bytes 16787712 | tf_op jit(solution)/shard_map/dot_general | solution.py:54
  309.9 2.9 scatter_custom_fusion.1
  312.9 19.7 %reduce-scatter.10.cloned.1.call-done = bf16[640,64]{1,0:T(8,128)(2,1)} async-done(((bf16[2560,64]{1,0:T(8,128)(2,1)}), bf16[640,64]{1,0:T(8,128)(2,1)}) %reduce-scatter.10.cloned.1.call-update) | async-done | bytes 81936
  336.0 8.4 %all-reduce.2 = (f32[64]{0:T(128)S(1)}, f32[64]{0:T(128)S(1)}) all-reduce(f32[64]{0:T(128)S(1)} %get-tuple-element.5, f32[64]{0:T(128)S(1)} %get-tuple-element.6), channel_id=1, replica_groups=mesh['segment'=2,'expert'=32,'tensor'=4] {'tensor'}, use_global_device_ids=true, to_apply=%region_3.4 | all-reduce | flops 128 | bytes 1024 | tf_op jit(solution)/shard_map/psum | solution.py:94
  344.5 2.8 gather_fusion.2
  348.6 35.6 %all_to_all.20 = bf16[2,32,12,640]{3,0,2,1:T(2,128)(2,1)S(1)} all-to-all(bf16[2,32,12,640]{3,0,2,1:T(2,128)(2,1)S(1)} %copy.59), channel_id=1, replica_groups=mesh['segment'=2,'expert'=32,'tensor'=4] {'expert'}, dimensions={1} | all-to-all | bytes 1966080 | tf_op jit(solution)/shard_map/all_to_all | solution.py:99
  387.5 18.2 %collective-permute-done.4 = bf16[2,384,640]{2,0,1:T(2,128)(2,1)S(1)} collective-permute-done((bf16[2,384,640]{2,0,1:T(2,128)(2,1)S(1)}, bf16[2,384,640]{2,0,1:T(2,128)(2,1)S(1)}, u32[]{:S(2)}, u32[]{:S(2)}) %collective-permute-start.4) | collective-permute-done | bytes 983072 | tf_op jit(solution)/shard_map/ppermute | solution.py:108
  408.4 17.1 %collective-permute-done.6 = bf16[2,384,640]{2,0,1:T(2,128)(2,1)} collective-permute-done((bf16[2,384,640]{2,0,1:T(2,128)(2,1)S(1)}, bf16[2,384,640]{2,0,1:T(2,128)(2,1)}, u32[]{:S(2)}, u32[]{:S(2)}) %collective-permute-start.6) | collective-permute-done | bytes 983072 | tf_op jit(solution)/shard_map/ppermute | solution.py:108
  431.0 10.5 %convolution_convert_fusion = bf16[2,384,2560]{2,1,0:T(8,128)(2,1)} fusion(bf16[2,384,2560]{2,1,0:T(8,128)(2,1)} %param.21, f32[2,384,384]{2,1,0:T(8,128)S(1)} %fusion.62, bf16[2,384,2560]{2,1,0:T(8,128)(2,1)} %copy-done.1, bf16[2,2560,384]{2,1,0:T(8,128)(2,1)} %param.20), kind=kOutput, calls=%fused_computation.6 | convolution fusion | flops 3023634432 | bytes 16908288 | tf_op jit(solution)/shard_map/lrh,lhd->lrd/dot_general | solution.py:123
  441.5 10.6 %copy.70 = bf16[2,384,2560]{1,0,2:T(2,128)(2,1)} copy(bf16[2,384,2560]{2,1,0:T(8,128)(2,1)} %convolution_convert_fusion) | data formatting | bytes 7864320
  452.1 4.7 copy.82
  456.9 2.9 scatter_custom_fusion
  459.8 2.8 gather_fusion
  463.9 31.1 %all_to_all.21 = bf16[2,32,12,640]{3,0,2,1:T(2,128)(2,1)S(1)} all-to-all(bf16[2,32,12,640]{3,0,2,1:T(2,128)(2,1)S(1)} %copy.46), channel_id=1, replica_groups=mesh['segment'=2,'expert'=32,'tensor'=4] {'expert'}, dimensions={1} | all-to-all | bytes 1966080 | tf_op jit(solution)/shard_map/all_to_all | solution.py:99
  495.0 3.2 collective-permute-start.2
  498.3 22.5 %collective-permute-done.1 = bf16[2,384,640]{2,0,1:T(2,128)(2,1)S(1)} collective-permute-done((bf16[2,384,640]{2,0,1:T(2,128)(2,1)S(1)}, bf16[2,384,640]{2,0,1:T(2,128)(2,1)S(1)}, u32[]{:S(2)}, u32[]{:S(2)}) %collective-permute-start.1) | collective-permute-done | bytes 983072 | tf_op jit(solution)/shard_map/ppermute | solution.py:108
  521.9 21.9 %collective-permute-done.3 = bf16[2,384,640]{2,0,1:T(2,128)(2,1)S(1)} collective-permute-done((bf16[2,384,640]{2,0,1:T(2,128)(2,1)S(1)}, bf16[2,384,640]{2,0,1:T(2,128)(2,1)S(1)}, u32[]{:S(2)}, u32[]{:S(2)}) %collective-permute-start.3) | collective-permute-done | bytes 983072 | tf_op jit(solution)/shard_map/ppermute | solution.py:108
  548.2 10.6 %convolution_convert_fusion.1 = bf16[2,384,2560]{2,1,0:T(8,128)(2,1)} fusion(bf16[2,384,2560]{2,1,0:T(8,128)(2,1)} %param.21, f32[2,384,384]{2,1,0:T(8,128)S(1)} %fusion.61, bf16[2,384,2560]{2,1,0:T(8,128)(2,1)} %copy-done, bf16[2,2560,384]{2,1,0:T(8,128)(2,1)} %param.20), kind=kOutput, calls=%fused_computation.7 | convolution fusion | flops 3023634432 | bytes 16908288 | tf_op jit(solution)/shard_map/lrh,lhd->lrd/dot_general | solution.py:123
  558.8 10.8 %copy.68 = bf16[2,384,2560]{1,0,2:T(2,128)(2,1)} copy(bf16[2,384,2560]{2,1,0:T(8,128)(2,1)} %convolution_convert_fusion.1) | data formatting | bytes 7864320
  569.6 4.7 copy.81
  576.6 2.8 copy.64
  579.4 10.4 %all-to-all-start.3 = ((bf16[2,32,12,640]{3,0,2,1:T(2,128)(2,1)}), bf16[2,32,12,640]{3,0,2,1:T(2,128)(2,1)S(1)}, u32[]{:S(2)}, u32[]{:S(2)}) async-start(bf16[2,32,12,640]{3,0,2,1:T(2,128)(2,1)} %bitcast.15), calls=%async_computation.3 | async-start | bytes 1966080 | tf_op jit(solution)/shard_map/all_to_all | solution.py:129
  589.8 30.8 %reduce-scatter.12.cloned.1.call-done = bf16[640,768]{1,0:T(8,128)(2,1)} async-done(((bf16[2560,768]{1,0:T(8,128)(2,1)}), bf16[640,768]{1,0:T(8,128)(2,1)}) %reduce-scatter.12.cloned.1.call-update) | async-done | bytes 983056
  623.0 2.9 copy.51
  625.8 10.4 %all-to-all-start.1 = ((bf16[2,32,12,640]{3,0,2,1:T(2,128)(2,1)}), bf16[2,32,12,640]{3,0,2,1:T(2,128)(2,1)S(1)}, u32[]{:S(2)}, u32[]{:S(2)}) async-start(bf16[2,32,12,640]{3,0,2,1:T(2,128)(2,1)} %bitcast.8), calls=%async_computation.1 | async-start | bytes 1966080 | tf_op jit(solution)/shard_map/all_to_all | solution.py:129
  638.7 2.8 gather_fusion.3
  642.7 20.7 %all-to-all-done.1 = bf16[2,32,12,640]{3,0,2,1:T(2,128)(2,1)S(1)} async-done(((bf16[2,32,12,640]{3,0,2,1:T(2,128)(2,1)}), bf16[2,32,12,640]{3,0,2,1:T(2,128)(2,1)S(1)}, u32[]{:S(2)}, u32[]{:S(2)}) %all-to-all-start.1) | async-done | bytes 983072 | tf_op jit(solution)/shard_map/all_to_all | solution.py:129
  (124 shorter events, 50.8 us)
Async XLA Ops:
  6.5 100.5 %all-gather.4.cloned.1.call-start = ((), (), s32[]{:S(2)}) async-start(), calls=%async_computation.7 | async-start | bytes 8110080 | tf_op jit(solution)/shard_map/all_gather | solution.py:45
  7.3 195.4 %all-gather.6.cloned.1.call-start = ((), (), s32[]{:S(2)}) async-start(), calls=%async_computation.8 | async-start | bytes 8110080 | tf_op jit(solution)/shard_map/all_gather | solution.py:50
  8.0 290.3 %all-gather.8.cloned.1.call-start = ((), (), s32[]{:S(2)}) async-start(), calls=%async_computation.9 | async-start | bytes 8110080 | tf_op jit(solution)/shard_map/all_gather | solution.py:56
  8.7 323.8 %reduce-scatter.10.cloned.1.call-start = ((), (), s32[]{:S(2)}) async-start(), calls=%async_computation.10 | async-start | bytes 819200
  27.0 271.3 %copy-start.5 = (f32[2560]{0:T(1024)S(1)}, f32[2560]{0:T(1024)}, u32[]{:S(2)}) copy-start(f32[2560]{0:T(1024)} %param.14) | copy-start | bytes 30724
  307.7 26.1 %copy-start.4 = (bf16[1,64,640]{2,1,0:T(8,128)(2,1)S(1)}, bf16[1,64,640]{2,1,0:T(8,128)(2,1)}, u32[]{:S(2)}) copy-start(bf16[1,64,640]{2,1,0:T(8,128)(2,1)} %param.11) | copy-start | bytes 245764
  309.6 264.7 %reduce-scatter.14.cloned.1.call-start = ((), (), s32[]{:S(2)}) async-start(), calls=%async_computation.12 | async-start | bytes 4915200
  309.9 34.6 %copy-start.9 = (s32[384]{0:T(512)}, s32[384]{0:T(512)S(1)}, u32[]{:S(2)}) copy-start(s32[384]{0:T(512)S(1)} %get-tuple-element.18) | copy-start | bytes 4612
  309.9 146.9 %copy-start.7 = (s32[384]{0:T(512)}, s32[384]{0:T(512)S(1)}, u32[]{:S(2)}) copy-start(s32[384]{0:T(512)S(1)} %get-tuple-element.17) | copy-start | bytes 4612
  333.8 1.4 collective-permute-start
  335.2 0.6 copy-start.2
  384.2 21.5 %collective-permute-start.4 = (bf16[2,384,640]{2,0,1:T(2,128)(2,1)S(1)}, bf16[2,384,640]{2,0,1:T(2,128)(2,1)S(1)}, u32[]{:S(2)}, u32[]{:S(2)}) collective-permute-start(bf16[2,384,640]{2,0,1:T(2,128)(2,1)S(1)} %bitcast.117), channel_id=1, source_target_pairs={{0,1},{1,2},{2,3},{3,0},{4,5},{5,6},{6,7},{7,4},{8,9},{9,10},{10,1... | collective-permute-start | bytes 2949128 | tf_op jit(solution)/shard_map/ppermute | solution.py:108
  385.6 22.5 %collective-permute-start.5 = (bf16[2,384,640]{2,0,1:T(2,128)(2,1)S(1)}, bf16[2,384,640]{2,0,1:T(2,128)(2,1)S(1)}, u32[]{:S(2)}, u32[]{:S(2)}) collective-permute-start(bf16[2,384,640]{2,0,1:T(2,128)(2,1)S(1)} %bitcast.118), channel_id=1, source_target_pairs={{0,3},{1,0},{2,1},{3,2},{4,7},{5,4},{6,5},{7,6},{8,11},{9,8},{10,9... | collective-permute-start | bytes 2949128 | tf_op jit(solution)/shard_map/ppermute | solution.py:111
  405.7 19.7 %collective-permute-start.6 = (bf16[2,384,640]{2,0,1:T(2,128)(2,1)S(1)}, bf16[2,384,640]{2,0,1:T(2,128)(2,1)}, u32[]{:S(2)}, u32[]{:S(2)}) collective-permute-start(bf16[2,384,640]{2,0,1:T(2,128)(2,1)S(1)} %collective-permute-done.4), channel_id=1, source_target_pairs={{0,1},{1,2},{2,3},{3,0},{4,5},{5,6},{6,7},{7,4},{8,9},{9,10},{10,1... | collective-permute-start | bytes 2949128 | tf_op jit(solution)/shard_map/ppermute | solution.py:108
  407.7 21.0 %copy-start.12 = (bf16[2,2560,384]{2,1,0:T(8,128)(2,1)S(1)}, bf16[2,2560,384]{2,1,0:T(8,128)(2,1)}, u32[]{:S(2)}) copy-start(bf16[2,2560,384]{2,1,0:T(8,128)(2,1)} %param.19) | copy-start | bytes 11796484
  426.9 1.9 copy-start.1
  456.8 163.9 %reduce-scatter.12.cloned.1.call-start = ((), (), s32[]{:S(2)}) async-start(), calls=%async_computation.11 | async-start | bytes 4915200
  495.0 25.8 %collective-permute-start.1 = (bf16[2,384,640]{2,0,1:T(2,128)(2,1)S(1)}, bf16[2,384,640]{2,0,1:T(2,128)(2,1)S(1)}, u32[]{:S(2)}, u32[]{:S(2)}) collective-permute-start(bf16[2,384,640]{2,0,1:T(2,128)(2,1)S(1)} %bitcast.120), channel_id=1, source_target_pairs={{0,1},{1,2},{2,3},{3,0},{4,5},{5,6},{6,7},{7,4},{8,9},{9,10},{10,1... | collective-permute-start | bytes 2949128 | tf_op jit(solution)/shard_map/ppermute | solution.py:108
  495.0 26.6 %collective-permute-start.2 = (bf16[2,384,640]{2,0,1:T(2,128)(2,1)S(1)}, bf16[2,384,640]{2,0,1:T(2,128)(2,1)S(1)}, u32[]{:S(2)}, u32[]{:S(2)}) collective-permute-start(bf16[2,384,640]{2,0,1:T(2,128)(2,1)S(1)} %bitcast.121), channel_id=1, source_target_pairs={{0,3},{1,0},{2,1},{3,2},{4,7},{5,4},{6,5},{7,6},{8,11},{9,8},{10,9... | collective-permute-start | bytes 2949128 | tf_op jit(solution)/shard_map/ppermute | solution.py:111
  520.8 23.0 %collective-permute-start.3 = (bf16[2,384,640]{2,0,1:T(2,128)(2,1)S(1)}, bf16[2,384,640]{2,0,1:T(2,128)(2,1)S(1)}, u32[]{:S(2)}, u32[]{:S(2)}) collective-permute-start(bf16[2,384,640]{2,0,1:T(2,128)(2,1)S(1)} %collective-permute-done.1), channel_id=1, source_target_pairs={{0,1},{1,2},{2,3},{3,0},{4,5},{5,6},{6,7},{7,4},{8,9},{9,10},{10,1... | collective-permute-start | bytes 2949128 | tf_op jit(solution)/shard_map/ppermute | solution.py:108
  521.2 24.8 %copy-start.13 = (bf16[2,2560,384]{2,1,0:T(8,128)(2,1)S(1)}, bf16[2,2560,384]{2,1,0:T(8,128)(2,1)}, u32[]{:S(2)}) copy-start(bf16[2,2560,384]{2,1,0:T(8,128)(2,1)} %param.19) | copy-start | bytes 11796484
  544.0 2.0 copy-start
  579.4 56.8 %copy-start.11 = (f32[2,64,6]{1,0,2:T(2,128)S(1)}, f32[2,64,6]{1,0,2:T(2,128)}, u32[]{:S(2)}) copy-start(f32[2,64,6]{1,0,2:T(2,128)} %param.13) | copy-start | bytes 9220
  579.4 57.6 %copy-start.10 = (s32[384]{0:T(512)S(1)}, s32[384]{0:T(512)}, u32[]{:S(2)}) copy-start(s32[384]{0:T(512)} %copy-done.9) | copy-start | bytes 4612
  579.4 58.2 %copy-start.8 = (s32[384]{0:T(512)S(1)}, s32[384]{0:T(512)}, u32[]{:S(2)}) copy-start(s32[384]{0:T(512)} %copy-done.7) | copy-start | bytes 4612
  579.4 46.4 %all-to-all-start.3 = ((bf16[2,32,12,640]{3,0,2,1:T(2,128)(2,1)}), bf16[2,32,12,640]{3,0,2,1:T(2,128)(2,1)S(1)}, u32[]{:S(2)}, u32[]{:S(2)}) async-start(bf16[2,32,12,640]{3,0,2,1:T(2,128)(2,1)} %bitcast.15), calls=%async_computation.3 | async-start | bytes 1966080 | tf_op jit(solution)/shard_map/all_to_all | solution.py:129
  625.8 37.5 %all-to-all-start.1 = ((bf16[2,32,12,640]{3,0,2,1:T(2,128)(2,1)}), bf16[2,32,12,640]{3,0,2,1:T(2,128)(2,1)S(1)}, u32[]{:S(2)}, u32[]{:S(2)}) async-start(bf16[2,32,12,640]{3,0,2,1:T(2,128)(2,1)} %bitcast.8), calls=%async_computation.1 | async-start | bytes 1966080 | tf_op jit(solution)/shard_map/all_to_all | solution.py:129
  666.8 4.1 copy-start.6
  666.8 6.0 copy-start.3
Sparse Core Ops, SparseCore 0:
  9.9 97.1 all-gather.3
  109.7 92.9 all-gather.5
  205.3 92.9 all-gather.7
  309.7 22.8 reduce-scatter.9
  456.9 48.3 reduce-scatter.13
  574.4 46.2 reduce-scatter.11
